TPU v7x, 32 devices: a whole 2x2x4 slice. The times are simulated.
32 devices in a mesh: dom: 8 (over z, x), section: 4 (over y, core).
Axes of the slice: x: 2, y: 2, z: 4, core: 2. Of those that a mesh axis runs over, the one named last changes fastest.
Arguments:
- node_latents: bfloat16 [4, 4, 8192, 128], P('section', None, 'dom'), may hold values from -6 to 6
- cotangent: bfloat16 [4, 8192, 128], P(None, 'dom'), may hold values from -6 to 6
- tile_weights: bfloat16 [64, 4, 128, 128], P('dom'), may hold values from -0.25 to 0.25
- tile_source: int32 [64, 4], P('dom'), may hold values from 0 to 11, as said below
- tile_count: int32 [64], P('dom'), may hold values from 2 to 4, as said below
- send_blocks: int32 [8, 2, 2], P('dom'), may hold values from 0 to 7, as said below
- w_message: bfloat16 [4, 128, 128], P('section'), may hold values from -0.5 to 0.5
- w_first: bfloat16 [4, 256, 128], P('section'), may hold values from -0.375 to 0.375
- bias_first: float32 [4, 128], P('section'), may hold values from -3 to 3
- w_second: bfloat16 [4, 128, 128], P('section'), may hold values from -0.5 to 0.5
- norm_gain: float32 [4, 128], P('section'), may hold values from 0.1 to 1.9
Outputs:
- grad_inputs: bfloat16 [4, 4, 8192, 128], P('section', None, 'dom')
- grad_message: float32 [4, 128, 128], P('section')
- grad_first: float32 [4, 256, 128], P('section')
- grad_bias: float32 [4, 128], P('section')
- grad_second: float32 [4, 128, 128], P('section')
- grad_gain: float32 [4, 128], P('section')
Inputs may be any that keep to these rules, and one draw needn't show every extreme that they name: `tile_source`: entries 0 to 7 name the subdomain's own blocks, 8 + j the j-th block received from the previous subdomain and 10 + j the j-th from the next; subdomains form a closed loop. Slot 0 of each block is the block itself. Only the first tile_count[b] slots of destination block b are live; the others are not part of the graph. `send_blocks`: the 2 blocks of one list are distinct.
All inputs are finite; a program needn't handle non-finite values.
Results may differ from a plain program's by a relative error of at most 0.025.
Values may be sent and summed in bfloat16 or wider, within the bound.
A program may use at most 64 MiB of HBM per device.

v0:
```python
import functools
import math

import jax
import jax.numpy as jnp
from jax import lax
from jax.experimental import pallas as pl
from jax.experimental.pallas import tpu as pltpu
from jax.sharding import PartitionSpec as P

epsilon = 1e-05
MESH = pl.DeviceIdType.MESH
F32 = jnp.float32
BF16 = jnp.bfloat16


def mm(a, b):
    return jnp.dot(a, b, preferred_element_type=F32)


def mm_nt(a, b):
    return lax.dot_general(a, b, (((1,), (1,)), ((), ())), preferred_element_type=F32)


def mm_tn(a, b):
    return lax.dot_general(a, b, (((0,), (0,)), ((), ())), preferred_element_type=F32)


def kernel(
    n,
    sections,
    chunk,
    normaliser,
    source_ref,
    count_ref,
    send_ref,
    latents_ref,
    cotangent_ref,
    tiles_ref,
    w_message_ref,
    w_first_ref,
    bias_ref,
    w_second_ref,
    gain_ref,
    out_ref,
    out_message_ref,
    out_first_ref,
    out_bias_ref,
    out_second_ref,
    out_gain_ref,
    incoming,
    messages,
    extended,
    outbox,
    dense,
    dense_t,
    aggregates,
    hiddens,
    normeds,
    inverses,
    factors,
    partial,
    grad_own,
    backbox,
    backs,
    totals,
    red_send,
    red_recv,
    gathered,
    cot_sem,
    out_send,
    out_recv,
    back_send,
    back_recv,
    sec_send,
    sec_recv,
    rs_send,
    rs_recv,
    ag_send,
    ag_recv,
):
    me = lax.axis_index("dom")
    section = lax.axis_index("section")
    is_last = section == sections - 1
    right, left = lax.rem(me + 1, n), lax.rem(me + n - 1, n)
    micros, rows, width = latents_ref.shape
    blocks, slots, size, _ = tiles_ref.shape
    entries = extended.shape[1]
    sends = (entries - blocks) // 2

    barrier = pltpu.get_barrier_semaphore()

    def greet(offset, carry):
        pl.semaphore_signal(
            barrier, inc=1, device_id=(lax.rem(me + offset, n), section), device_id_type=MESH
        )
        return carry

    lax.fori_loop(1, n, greet, 0)

    @pl.when(section > 0)
    def _():
        pl.semaphore_signal(barrier, inc=1, device_id=(me, section - 1), device_id_type=MESH)

    @pl.when(jnp.logical_not(is_last))
    def _():
        pl.semaphore_signal(barrier, inc=1, device_id=(me, section + 1), device_id_type=MESH)

    cot_copy = pltpu.make_async_copy(cotangent_ref, incoming, cot_sem)

    @pl.when(is_last)
    def _():
        cot_copy.start()

    def make_messages(m, carry):
        value = mm(latents_ref[m], w_message_ref[...]).astype(BF16)
        value = value.reshape(blocks, size, width)
        extended[m, 0:blocks] = value
        messages[...] = value
        for side in range(2):
            for j in range(sends):
                outbox[m, side, j] = messages[send_ref[side * sends + j]]
        return carry

    lax.fori_loop(0, micros, make_messages, 0)
    pl.semaphore_wait(
        barrier, n - 1 + jnp.where(section > 0, 1, 0) + jnp.where(is_last, 0, 1)
    )

    def halo_copy(m, side):
        start = blocks + (0 if side == 1 else sends)
        return pltpu.make_async_remote_copy(
            src_ref=outbox.at[m, side],
            dst_ref=extended.at[m, pl.ds(start, sends)],
            send_sem=out_send.at[m, side],
            recv_sem=out_recv.at[m, side],
            device_id=(right if side == 1 else left, section),
            device_id_type=MESH,
        )

    def back_copy(m, side):
        return pltpu.make_async_remote_copy(
            src_ref=backbox.at[m, side],
            dst_ref=backs.at[m, side],
            send_sem=back_send.at[m, side],
            recv_sem=back_recv.at[m, side],
            device_id=(left if side == 0 else right, section),
            device_id_type=MESH,
        )

    def section_copy(m):
        return pltpu.make_async_remote_copy(
            src_ref=out_ref.at[m],
            dst_ref=incoming.at[m],
            send_sem=sec_send.at[m],
            recv_sem=sec_recv.at[m],
            device_id=(me, section - 1),
            device_id_type=MESH,
        )

    def start_halo(m, carry):
        halo_copy(m, 0).start()
        halo_copy(m, 1).start()
        return carry

    lax.fori_loop(0, micros, start_halo, 0)

    def build(b, carry):
        live = [k < count_ref[b] for k in range(slots)]
        tiles = [tiles_ref[b, k].astype(F32) for k in range(slots)]
        flipped = [tile.T for tile in tiles]
        column = pl.ds(pl.multiple_of(b * size, size), size)
        for e in range(entries):
            value = jnp.zeros((size, size), F32)
            value_t = jnp.zeros((size, size), F32)
            for k in range(slots):
                hit = jnp.logical_and(source_ref[b * slots + k] == e, live[k])
                weight = jnp.where(hit, 1.0, 0.0).astype(F32)
                value = value + tiles[k] * weight
                value_t = value_t + flipped[k] * weight
            dense[b, :, e * size : (e + 1) * size] = value.astype(BF16)
            dense_t[e * size : (e + 1) * size, column] = value_t.astype(BF16)
        return carry

    lax.fori_loop(0, blocks, build, 0)

    totals[...] = jnp.zeros_like(totals)

    def forward(m):
        halo_copy(m, 0).wait()
        halo_copy(m, 1).wait()
        coupling = dense[...].reshape(rows, entries * size)
        aggregate = mm(coupling, extended[m].reshape(entries * size, width)).astype(BF16)
        aggregates[m] = aggregate
        joined = jnp.concatenate([latents_ref[m], aggregate], axis=1)
        before = mm(joined, w_first_ref[...]) + bias_ref[...]
        sigmoid = 1.0 / (1.0 + jnp.exp(-before))
        hidden = (before * sigmoid).astype(BF16)
        hiddens[m] = hidden
        factors[m] = sigmoid * (1.0 + before * (1.0 - sigmoid))
        output = mm(hidden, w_second_ref[...])
        centred = output - jnp.mean(output, axis=-1, keepdims=True)
        inverse = lax.rsqrt(jnp.mean(centred * centred, axis=-1, keepdims=True) + epsilon)
        normeds[m] = centred * inverse
        inverses[m] = inverse

    def upfront(m, carry):
        forward(m)
        return carry

    lax.fori_loop(0, jnp.where(is_last, 1, micros), upfront, 0)

    @pl.when(is_last)
    def _():
        cot_copy.wait()

    def turn(m, carry):
        @pl.when(jnp.logical_not(is_last))
        def _():
            section_copy(m).wait_recv()

        value = incoming[m].astype(F32)
        normed = normeds[m]
        gain_row = jnp.sum(value * normed, axis=0, keepdims=True)
        scaled = value * gain_ref[...]
        grad_out = inverses[m] * (
            scaled
            - jnp.mean(scaled, axis=-1, keepdims=True)
            - normed * jnp.mean(scaled * normed, axis=-1, keepdims=True)
        )
        grad_out = grad_out.astype(BF16)
        grad_before = (mm_nt(grad_out, w_second_ref[...]) * factors[m]).astype(BF16)
        grad_joined = mm_nt(grad_before, w_first_ref[...])
        partial[...] = value + grad_joined[:, :width]
        grad_aggregate = grad_joined[:, width:].astype(BF16)
        rim = mm(dense_t[blocks * size :, :], grad_aggregate).astype(BF16)
        backbox[m] = rim.reshape(2, sends, size, width)
        back_copy(m, 0).start()
        back_copy(m, 1).start()
        own = mm(dense_t[: blocks * size, :], grad_aggregate)
        grad_own[...] = own.reshape(blocks, size, width)
        joined = jnp.concatenate([latents_ref[m], aggregates[m]], axis=1)
        totals[width : 3 * width] += mm_tn(joined, grad_before)
        totals[3 * width : 4 * width] += mm_tn(hiddens[m], grad_out)
        bias_row = jnp.sum(grad_before.astype(F32), axis=0, keepdims=True)
        totals[4 * width : 4 * width + 1] += bias_row
        totals[4 * width + 1 : 4 * width + 2] += gain_row

        ahead = jnp.where(is_last, jnp.minimum(m + 2, micros), m + 1)
        lax.fori_loop(m + 1, ahead, upfront, 0)

        back_copy(m, 0).wait()
        back_copy(m, 1).wait()
        pieces = []
        for i in range(blocks):
            piece = grad_own[i]
            for j in range(sends):
                to_next = jnp.where(send_ref[sends + j] == i, 1.0, 0.0).astype(F32)
                to_previous = jnp.where(send_ref[j] == i, 1.0, 0.0).astype(F32)
                piece = piece + backs[m, 0, j].astype(F32) * to_next
                piece = piece + backs[m, 1, j].astype(F32) * to_previous
            pieces.append(piece.astype(BF16))
        grad_messages = jnp.concatenate(pieces, axis=0)
        result = partial[...] + mm_nt(grad_messages, w_message_ref[...])
        out_ref[m] = result.astype(BF16)

        @pl.when(section > 0)
        def _():
            section_copy(m).start()

        totals[0:width] += mm_tn(latents_ref[m], grad_messages)
        return carry

    lax.fori_loop(0, micros, turn, 0)

    red_send[...] = totals[...].astype(BF16)

    def part(index):
        return pl.ds(pl.multiple_of(index * chunk, 16), chunk)

    def rs_copy(offset):
        peer = lax.rem(me + offset, n)
        return pltpu.make_async_remote_copy(
            src_ref=red_send.at[part(peer)],
            dst_ref=red_recv.at[offset - 1],
            send_sem=rs_send.at[offset - 1],
            recv_sem=rs_recv.at[offset - 1],
            device_id=(peer, section),
            device_id_type=MESH,
        )

    def ag_copy(offset):
        return pltpu.make_async_remote_copy(
            src_ref=gathered.at[part(me)],
            dst_ref=gathered.at[part(me)],
            send_sem=ag_send.at[offset - 1],
            recv_sem=ag_recv.at[offset - 1],
            device_id=(lax.rem(me + offset, n), section),
            device_id_type=MESH,
        )

    def ag_arrival(offset):
        owner = lax.rem(me + n - offset, n)
        return pltpu.make_async_remote_copy(
            src_ref=gathered.at[part(owner)],
            dst_ref=gathered.at[part(owner)],
            send_sem=ag_send.at[offset - 1],
            recv_sem=ag_recv.at[offset - 1],
            device_id=(lax.rem(me + offset, n), section),
            device_id_type=MESH,
        )

    def each(body):
        def step(offset, carry):
            body(offset)
            return carry

        lax.fori_loop(1, n, step, 0)

    each(lambda offset: rs_copy(offset).start())

    def collect(offset, total):
        rs_copy(offset).wait()
        return total + red_recv[offset - 1].astype(F32)

    total = lax.fori_loop(1, n, collect, totals[part(me), :])
    gathered[part(me), :] = (total * normaliser).astype(BF16)
    each(lambda offset: ag_copy(offset).start())

    def finish_section(m, carry):
        section_copy(m).wait_send()
        return carry

    @pl.when(section > 0)
    def _():
        lax.fori_loop(0, micros, finish_section, 0)

    each(lambda offset: ag_arrival(offset).wait_recv())
    each(lambda offset: ag_copy(offset).wait_send())
    out_message_ref[...] = gathered[0:width].astype(F32)
    out_first_ref[...] = gathered[width : 3 * width].astype(F32)
    out_second_ref[...] = gathered[3 * width : 4 * width].astype(F32)
    tail = gathered[4 * width : 4 * width + 16].astype(F32)
    out_bias_ref[...] = tail[0:1]
    out_gain_ref[...] = tail[1:2]


def per_device(
    n,
    sections,
    node_latents,
    cotangent,
    tile_weights,
    tile_source,
    tile_count,
    send_blocks,
    w_message,
    w_first,
    bias_first,
    w_second,
    norm_gain,
):
    micros, rows, width = cotangent.shape
    blocks, slots, size, _ = tile_weights.shape
    sends = send_blocks.shape[2]
    entries = blocks + 2 * sends
    total_rows = 4 * width + 16
    chunk = -(-total_rows // (16 * n)) * 16
    normaliser = 1.0 / math.sqrt(micros * rows * n)
    vmem = pl.BlockSpec(memory_space=pltpu.VMEM)
    smem = pl.BlockSpec(memory_space=pltpu.SMEM)
    dma = pltpu.SemaphoreType.DMA
    results = pl.pallas_call(
        functools.partial(kernel, n, sections, chunk, normaliser),
        out_shape=(
            jax.ShapeDtypeStruct((micros, rows, width), BF16),
            jax.ShapeDtypeStruct((width, width), F32),
            jax.ShapeDtypeStruct((2 * width, width), F32),
            jax.ShapeDtypeStruct((1, width), F32),
            jax.ShapeDtypeStruct((width, width), F32),
            jax.ShapeDtypeStruct((1, width), F32),
        ),
        in_specs=[smem] * 3 + [vmem, pl.BlockSpec(memory_space=pl.ANY)] + [vmem] * 6,
        out_specs=(vmem,) * 6,
        scratch_shapes=[
            pltpu.VMEM((micros, rows, width), BF16),
            pltpu.VMEM((blocks, size, width), BF16),
            pltpu.VMEM((micros, entries, size, width), BF16),
            pltpu.VMEM((micros, 2, sends, size, width), BF16),
            pltpu.VMEM((blocks, size, entries * size), BF16),
            pltpu.VMEM((entries * size, blocks * size), BF16),
            pltpu.VMEM((micros, rows, width), BF16),
            pltpu.VMEM((micros, rows, width), BF16),
            pltpu.VMEM((micros, rows, width), F32),
            pltpu.VMEM((micros, rows, 1), F32),
            pltpu.VMEM((micros, rows, width), F32),
            pltpu.VMEM((rows, width), F32),
            pltpu.VMEM((blocks, size, width), F32),
            pltpu.VMEM((micros, 2, sends, size, width), BF16),
            pltpu.VMEM((micros, 2, sends, size, width), BF16),
            pltpu.VMEM((n * chunk, width), F32),
            pltpu.VMEM((n * chunk, width), BF16),
            pltpu.VMEM((n - 1, chunk, width), BF16),
            pltpu.VMEM((n * chunk, width), BF16),
            dma(()),
            dma((micros, 2)),
            dma((micros, 2)),
            dma((micros, 2)),
            dma((micros, 2)),
            dma((micros,)),
            dma((micros,)),
            dma((n - 1,)),
            dma((n - 1,)),
            dma((n - 1,)),
            dma((n - 1,)),
        ],
        compiler_params=pltpu.CompilerParams(
            collective_id=0, has_side_effects=True, vmem_limit_bytes=56 * 1024 * 1024
        ),
    )(
        tile_source.reshape(-1),
        tile_count,
        send_blocks.reshape(-1),
        node_latents[0],
        cotangent,
        tile_weights,
        w_message[0],
        w_first[0],
        bias_first,
        w_second[0],
        norm_gain,
    )
    grads, message, first, bias, second, gain = results
    return (grads[None], message[None], first[None], bias, second[None], gain)


def solution(mesh):
    return jax.shard_map(
        functools.partial(per_device, mesh.shape["dom"], mesh.shape["section"]),
        mesh=mesh,
        in_specs=(
            P("section", None, "dom", None),
            P(None, "dom", None),
            P("dom", None, None, None),
            P("dom", None),
            P("dom"),
            P("dom", None, None),
            P("section", None, None),
            P("section", None, None),
            P("section", None),
            P("section", None, None),
            P("section", None),
        ),
        out_specs=(
            P("section", None, "dom", None),
            P("section", None, None),
            P("section", None, None),
            P("section", None),
            P("section", None, None),
            P("section", None),
        ),
        check_vma=False,
    )
```

profile of v0, /device:TPU:0, one launch (start us, length us, event | category | flops | bytes accessed | tf_op | source)
XLA Modules:
  0.0 87.9 jit_solution(697188335525802512)
XLA Ops:
  0.6 0.0 copy-start.4
  0.6 0.0 copy-start.3
  0.7 0.7 copy-done.4
  1.3 0.6 reshape.19.send_ref
  1.9 0.0 copy-done.3
  1.9 0.1 copy.18
  2.0 0.6 reshape.18.source_ref
  2.6 79.7 %shard_map.154 = (bf16[4,1024,128]{2,1,0:T(8,128)(2,1)}, f32[128,128]{1,0:T(8,128)}, f32[256,128]{1,0:T(8,128)}, f32[1,128]{1,0:T(1,128)}, f32[128,128]{1,0:T(8,128)}, /*index=5*/f32[1,128]{1,0:T(1,128)}) custom-call(s32[32]{0:T(128)} %reshape.18.source_ref, s32[8]{0:T(128)} %count_ref.1, s32[4]{0:T(128)} %reshape.19.send_ref, ...), custom_call_target="tpu_custom_call" | custom-call | tf_op jit(solution)/shard_map/pallas_call | solution.py:373
  82.3 0.0 copy-start.2
  82.3 2.3 %copy.25 = bf16[1,4,1024,128]{3,2,1,0:T(8,128)(2,1)} copy(bf16[1,4,1024,128]{3,2,1,0:T(8,128)(2,1)} %bitcast.9) | data formatting | bytes 2097152
  84.6 0.0 copy-done.2
  84.6 0.0 copy-start
  84.6 0.6 copy.26
  85.3 0.3 copy-done
  85.5 0.0 copy-start.6
  85.6 0.0 copy-start.1
  85.6 0.7 copy.27
  86.2 0.0 copy-done.6
  86.2 0.5 copy.28
  86.7 0.0 copy-done.1
  86.7 0.0 copy-start.5
  86.7 0.6 copy.29
  87.4 0.0 copy-done.5
  87.4 0.5 copy.30
Async XLA Ops:
  0.6 0.7 copy-start.4
  0.6 1.3 %copy-start.3 = (s32[8,4]{0,1:T(4,128)S(1)}, s32[8,4]{0,1:T(4,128)}, u32[]{:S(2)}) copy-start(s32[8,4]{0,1:T(4,128)} %param.14) | copy-start | bytes 388
  82.3 2.3 %copy-start.2 = (f32[128,128]{1,0:T(8,128)S(1)}, f32[128,128]{1,0:T(8,128)}, u32[]{:S(2)}) copy-start(f32[128,128]{1,0:T(8,128)} %get-tuple-element.13) | copy-start | bytes 196612
  84.6 0.9 %copy-start = (f32[256,128]{1,0:T(8,128)S(1)}, f32[256,128]{1,0:T(8,128)}, u32[]{:S(2)}) copy-start(f32[256,128]{1,0:T(8,128)} %get-tuple-element.14) | copy-start | bytes 393220
  85.5 0.7 copy-start.6
  85.6 1.2 %copy-start.1 = (f32[128,128]{1,0:T(8,128)S(1)}, f32[128,128]{1,0:T(8,128)}, u32[]{:S(2)}) copy-start(f32[128,128]{1,0:T(8,128)} %get-tuple-element.16) | copy-start | bytes 196612
  86.7 0.7 copy-start.5
where the time goes:
time: 88.2 us; the launch traced here: 87.9 us
  Pallas kernels  79.7 us (90%)
  local copies, waits for them, and re-layouts  7.51 us (9%)
    pallas_call x1, Pallas kernels, per_device(): pl.pallas_call(functools.partial(kernel, n, sections, chunk, normaliser),...  79.7 us
    unnamed x21, local copies, waits for them, and re-layouts  6.32 us

commit v1 on v0

v1 whole, which is shorter than its diff:
```python
import functools
import math

import jax
import jax.numpy as jnp
from jax import lax
from jax.experimental import pallas as pl
from jax.experimental.pallas import tpu as pltpu
from jax.sharding import PartitionSpec as P

epsilon = 1e-05
MESH = pl.DeviceIdType.MESH
F32 = jnp.float32
BF16 = jnp.bfloat16
parts = 2


def mm(a, b):
    return jnp.dot(a, b, preferred_element_type=F32)


def mm_nt(a, b):
    return lax.dot_general(a, b, (((1,), (1,)), ((), ())), preferred_element_type=F32)


def mm_tn(a, b):
    return lax.dot_general(a, b, (((0,), (0,)), ((), ())), preferred_element_type=F32)


def kernel(
    n,
    sections,
    chunks,
    normaliser,
    source_ref,
    count_ref,
    send_ref,
    latents_hbm,
    cotangent_ref,
    tiles_hbm,
    w_message_hbm,
    w_first_hbm,
    bias_hbm,
    w_second_hbm,
    gain_hbm,
    out_ref,
    gathered_a,
    gathered_b,
    w_message_ref,
    w_first_ref,
    bias_ref,
    w_second_ref,
    gain_ref,
    weight_sem,
    latents_ref,
    tiles_ref,
    incoming,
    messages,
    extended,
    outbox,
    dense,
    dense_t,
    aggregates,
    hiddens,
    normeds,
    inverses,
    factors,
    partial,
    grad_own,
    grad_outs,
    grad_befores,
    grad_aggregates,
    backbox,
    backs,
    totals,
    message_total,
    send_a,
    recv_a,
    send_b,
    recv_b,
    cot_sem,
    latents_sem,
    tiles_sem,
    out_send,
    out_recv,
    back_send,
    back_recv,
    sec_send,
    sec_recv,
    rs_send_a,
    rs_recv_a,
    ag_send_a,
    ag_recv_a,
    rs_send_b,
    rs_recv_b,
    ag_send_b,
    ag_recv_b,
):
    me = lax.axis_index("dom")
    section = lax.axis_index("section")
    is_last = section == sections - 1
    right, left = lax.rem(me + 1, n), lax.rem(me + n - 1, n)
    micros, rows, width = latents_ref.shape
    blocks, slots, size, _ = tiles_ref.shape
    entries = extended.shape[1]
    sends = (entries - blocks) // 2

    barrier = pltpu.get_barrier_semaphore()

    def greet(offset, carry):
        pl.semaphore_signal(
            barrier, inc=1, device_id=(lax.rem(me + offset, n), section), device_id_type=MESH
        )
        return carry

    lax.fori_loop(1, n, greet, 0)

    @pl.when(section > 0)
    def _():
        pl.semaphore_signal(barrier, inc=1, device_id=(me, section - 1), device_id_type=MESH)

    @pl.when(jnp.logical_not(is_last))
    def _():
        pl.semaphore_signal(barrier, inc=1, device_id=(me, section + 1), device_id_type=MESH)

    def latents_copy(m):
        return pltpu.make_async_copy(latents_hbm.at[m], latents_ref.at[m], latents_sem.at[m])

    message_copy = pltpu.make_async_copy(w_message_hbm, w_message_ref, weight_sem.at[0])
    weight_copies = [
        pltpu.make_async_copy(w_first_hbm, w_first_ref, weight_sem.at[1]),
        pltpu.make_async_copy(bias_hbm, bias_ref, weight_sem.at[2]),
        pltpu.make_async_copy(w_second_hbm, w_second_ref, weight_sem.at[3]),
        pltpu.make_async_copy(gain_hbm, gain_ref, weight_sem.at[4]),
    ]
    message_copy.start()
    for m in range(micros):
        latents_copy(m).start()
    for copy in weight_copies:
        copy.start()
    tiles_copy = pltpu.make_async_copy(tiles_hbm, tiles_ref, tiles_sem)
    tiles_copy.start()

    cot_copy = pltpu.make_async_copy(cotangent_ref, incoming, cot_sem)

    @pl.when(is_last)
    def _():
        cot_copy.start()

    def make_messages(m, carry):
        latents_copy(m).wait()
        value = mm(latents_ref[m], w_message_ref[...]).astype(BF16)
        value = value.reshape(blocks, size, width)
        extended[m, 0:blocks] = value
        messages[...] = value
        for side in range(2):
            for j in range(sends):
                outbox[m, side, j] = messages[send_ref[side, j]]
        return carry

    message_copy.wait()
    make_messages(0, 0)
    pl.semaphore_wait(
        barrier, n - 1 + jnp.where(section > 0, 1, 0) + jnp.where(is_last, 0, 1)
    )

    def halo_copy(m, side):
        start = blocks + (0 if side == 1 else sends)
        return pltpu.make_async_remote_copy(
            src_ref=outbox.at[m, side],
            dst_ref=extended.at[m, pl.ds(start, sends)],
            send_sem=out_send.at[m, side],
            recv_sem=out_recv.at[m, side],
            device_id=(right if side == 1 else left, section),
            device_id_type=MESH,
        )

    def back_copy(m, side):
        return pltpu.make_async_remote_copy(
            src_ref=backbox.at[m, side],
            dst_ref=backs.at[m, side],
            send_sem=back_send.at[m, side],
            recv_sem=back_recv.at[m, side],
            device_id=(left if side == 0 else right, section),
            device_id_type=MESH,
        )

    part_rows = rows // parts

    def section_copy(m, q):
        span = pl.ds(q * part_rows, part_rows)
        return pltpu.make_async_remote_copy(
            src_ref=out_ref.at[m, span],
            dst_ref=incoming.at[m, span],
            send_sem=sec_send.at[m, q],
            recv_sem=sec_recv.at[m, q],
            device_id=(me, section - 1),
            device_id_type=MESH,
        )

    def start_halo(m, carry):
        halo_copy(m, 0).start()
        halo_copy(m, 1).start()
        return carry

    start_halo(0, 0)
    lax.fori_loop(1, micros, make_messages, 0)
    start_halo(1, 0)
    for copy in weight_copies:
        copy.wait()
    tiles_copy.wait()

    def build(b, carry):
        live = [k < count_ref[b] for k in range(slots)]
        tiles = [tiles_ref[b, k].astype(F32) for k in range(slots)]
        flipped = [tile.T for tile in tiles]
        column = pl.ds(pl.multiple_of(b * size, size), size)
        for e in range(entries):
            value = jnp.zeros((size, size), F32)
            value_t = jnp.zeros((size, size), F32)
            for k in range(slots):
                hit = jnp.logical_and(source_ref[k, b] == e, live[k])
                weight = jnp.where(hit, 1.0, 0.0).astype(F32)
                value = value + tiles[k] * weight
                value_t = value_t + flipped[k] * weight
            dense[b, :, e * size : (e + 1) * size] = value.astype(BF16)
            dense_t[e * size : (e + 1) * size, column] = value_t.astype(BF16)
        return carry

    lax.fori_loop(0, blocks, build, 0)

    totals[...] = jnp.zeros_like(totals)
    message_total[...] = jnp.zeros_like(message_total)

    def forward(m):
        halo_copy(m, 0).wait_recv()
        halo_copy(m, 1).wait_recv()
        lax.fori_loop(jnp.minimum(m + 2, micros), jnp.minimum(m + 3, micros), start_halo, 0)
        coupling = dense[...].reshape(rows, entries * size)
        aggregate = mm(coupling, extended[m].reshape(entries * size, width)).astype(BF16)
        aggregates[m] = aggregate
        joined = jnp.concatenate([latents_ref[m], aggregate], axis=1)
        before = mm(joined, w_first_ref[...]) + bias_ref[...]
        sigmoid = 1.0 / (1.0 + jnp.exp(-before))
        hidden = (before * sigmoid).astype(BF16)
        hiddens[m] = hidden
        factors[m] = sigmoid * (1.0 + before * (1.0 - sigmoid))
        output = mm(hidden, w_second_ref[...])
        centred = output - jnp.mean(output, axis=-1, keepdims=True)
        inverse = lax.rsqrt(jnp.mean(centred * centred, axis=-1, keepdims=True) + epsilon)
        normeds[m] = centred * inverse
        inverses[m] = inverse

    def upfront(m, carry):
        forward(m)
        return carry

    @pl.when(is_last)
    def _():
        cot_copy.wait()

    def row_part(index, chunk):
        return pl.ds(pl.multiple_of(index * chunk, 16), chunk)

    def reduction(chunk, source, landing, result, sems):
        rs_send, rs_recv, ag_send, ag_recv = sems

        def rs_copy(offset):
            peer = lax.rem(me + offset, n)
            return pltpu.make_async_remote_copy(
                src_ref=source.at[row_part(peer, chunk)],
                dst_ref=landing.at[offset - 1],
                send_sem=rs_send.at[offset - 1],
                recv_sem=rs_recv.at[offset - 1],
                device_id=(peer, section),
                device_id_type=MESH,
            )

        def ag_copy(offset, owner):
            return pltpu.make_async_remote_copy(
                src_ref=result.at[row_part(owner, chunk)],
                dst_ref=result.at[row_part(owner, chunk)],
                send_sem=ag_send.at[offset - 1],
                recv_sem=ag_recv.at[offset - 1],
                device_id=(lax.rem(me + offset, n), section),
                device_id_type=MESH,
            )

        def each(body):
            def step(offset, carry):
                body(offset)
                return carry

            lax.fori_loop(1, n, step, 0)

        def scatter(total):
            source[...] = total[...].astype(BF16)
            each(lambda offset: rs_copy(offset).start())

        def gather(total):
            def collect(offset, value):
                rs_copy(offset).wait()
                return value + landing[offset - 1].astype(F32)

            value = lax.fori_loop(1, n, collect, total[row_part(me, chunk), :])
            result[row_part(me, chunk), :] = (value * normaliser).astype(BF16)
            each(lambda offset: ag_copy(offset, me).start())

        def finish():
            each(lambda offset: ag_copy(offset, lax.rem(me + n - offset, n)).wait_recv())
            each(lambda offset: ag_copy(offset, me).wait_send())

        return scatter, gather, finish

    scatter_a, gather_a, finish_a = reduction(
        chunks[0], send_a, recv_a, gathered_a, (rs_send_a, rs_recv_a, ag_send_a, ag_recv_a)
    )
    scatter_b, gather_b, finish_b = reduction(
        chunks[1], send_b, recv_b, gathered_b, (rs_send_b, rs_recv_b, ag_send_b, ag_recv_b)
    )

    def first_half(m, carry):
        slot = lax.rem(m, 2)
        gain_row = jnp.zeros((1, width), F32)
        bias_row = jnp.zeros((1, width), F32)
        for q in range(parts):
            span = slice(q * part_rows, (q + 1) * part_rows)

            @pl.when(jnp.logical_not(is_last))
            def _():
                section_copy(m, q).wait_recv()

            value = incoming[m, span].astype(F32)
            normed = normeds[m, span]
            gain_row += jnp.sum(value * normed, axis=0, keepdims=True)
            scaled = value * gain_ref[...]
            grad_out = inverses[m, span] * (
                scaled
                - jnp.mean(scaled, axis=-1, keepdims=True)
                - normed * jnp.mean(scaled * normed, axis=-1, keepdims=True)
            )
            grad_out = grad_out.astype(BF16)
            grad_outs[span] = grad_out
            grad_before = (mm_nt(grad_out, w_second_ref[...]) * factors[m, span]).astype(BF16)
            grad_befores[span] = grad_before
            bias_row += jnp.sum(grad_before.astype(F32), axis=0, keepdims=True)
            grad_joined = mm_nt(grad_before, w_first_ref[...])
            partial[slot, span] = value + grad_joined[:, :width]
            grad_aggregates[span] = grad_joined[:, width:].astype(BF16)
        for side in range(2):
            start = (blocks + side * sends) * size
            rim = mm(dense_t[start : start + sends * size, :], grad_aggregates[...])
            backbox[m, side] = rim.astype(BF16).reshape(sends, size, width)
            back_copy(m, side).start()
        own = mm(dense_t[: blocks * size, :], grad_aggregates[...])
        grad_own[slot] = own.reshape(blocks, size, width)
        joined = jnp.concatenate([latents_ref[m], aggregates[m]], axis=1)
        totals[: 2 * width] += mm_tn(joined, grad_befores[...])
        totals[2 * width : 3 * width] += mm_tn(hiddens[m], grad_outs[...])
        totals[3 * width : 3 * width + 1] += bias_row
        totals[3 * width + 1 : 3 * width + 2] += gain_row

        return carry

    def second_half(m, carry):
        slot = lax.rem(m, 2)
        back_copy(m, 0).wait_recv()
        back_copy(m, 1).wait_recv()
        for q in range(parts):
            span = slice(q * part_rows, (q + 1) * part_rows)
            pieces = []
            for i in range(q * blocks // parts, (q + 1) * blocks // parts):
                piece = grad_own[slot, i]
                for j in range(sends):
                    to_next = jnp.where(send_ref[1, j] == i, 1.0, 0.0).astype(F32)
                    to_previous = jnp.where(send_ref[0, j] == i, 1.0, 0.0).astype(F32)
                    piece = piece + backs[m, 0, j].astype(F32) * to_next
                    piece = piece + backs[m, 1, j].astype(F32) * to_previous
                pieces.append(piece.astype(BF16))
            grad_messages = jnp.concatenate(pieces, axis=0)
            grad_outs[span] = grad_messages
            result = partial[slot, span] + mm_nt(grad_messages, w_message_ref[...])
            out_ref[m, span] = result.astype(BF16)

            @pl.when(section > 0)
            def _():
                section_copy(m, q).start()

        message_total[0:width] += mm_tn(latents_ref[m], grad_outs[...])
        return carry

    def turn(t, carry):
        start = jnp.where(is_last, t, jnp.where(t == 0, 0, micros))
        stop = jnp.where(is_last, jnp.minimum(t + 1, micros), micros)
        lax.fori_loop(start, stop, upfront, 0)
        lax.fori_loop(t, jnp.minimum(t + 1, micros), first_half, 0)

        @pl.when(t == micros)
        def _():
            scatter_a(totals)

        lax.fori_loop(jnp.maximum(t - 1, 0), t, second_half, 0)
        return carry

    lax.fori_loop(0, micros + 1, turn, 0)
    scatter_b(message_total)
    gather_a(totals)
    gather_b(message_total)

    def finish_halos(m, carry):
        for side in range(2):
            halo_copy(m, side).wait_send()
            back_copy(m, side).wait_send()
        return carry

    lax.fori_loop(0, micros, finish_halos, 0)

    def finish_section(m, carry):
        for q in range(parts):
            section_copy(m, q).wait_send()
        return carry

    @pl.when(section > 0)
    def _():
        lax.fori_loop(0, micros, finish_section, 0)

    finish_a()
    finish_b()


def unpack(grads_ref, a_ref, b_ref, out_ref, message_ref, first_ref, bias_ref, second_ref, gain_ref, sem):
    width = message_ref.shape[-1]
    copy = pltpu.make_async_copy(grads_ref, out_ref, sem)
    copy.start()
    message_ref[...] = b_ref[0:width].astype(F32)
    first_ref[...] = a_ref[0 : 2 * width].astype(F32)
    second_ref[...] = a_ref[2 * width : 3 * width].astype(F32)
    tail = a_ref[3 * width : 3 * width + 16].astype(F32)
    bias_ref[...] = tail[0:1]
    gain_ref[...] = tail[1:2]
    copy.wait()


def per_device(
    n,
    sections,
    node_latents,
    cotangent,
    tile_weights,
    tile_source,
    tile_count,
    send_blocks,
    w_message,
    w_first,
    bias_first,
    w_second,
    norm_gain,
):
    micros, rows, width = cotangent.shape
    blocks, slots, size, _ = tile_weights.shape
    sends = send_blocks.shape[2]
    entries = blocks + 2 * sends
    chunk_a = -(-(3 * width + 16) // (16 * n)) * 16
    chunk_b = -(-width // (16 * n)) * 16
    normaliser = 1.0 / math.sqrt(micros * rows * n)
    vmem = pl.BlockSpec(memory_space=pltpu.VMEM)
    smem = pl.BlockSpec(memory_space=pltpu.SMEM)
    anywhere = pl.BlockSpec(memory_space=pl.ANY)
    hbm = pl.BlockSpec(memory_space=pltpu.HBM)
    dma = pltpu.SemaphoreType.DMA
    grads, packed_a, packed_b = pl.pallas_call(
        functools.partial(kernel, n, sections, (chunk_a, chunk_b), normaliser),
        out_shape=(
            jax.ShapeDtypeStruct((micros, rows, width), BF16),
            jax.ShapeDtypeStruct((n * chunk_a, width), BF16),
            jax.ShapeDtypeStruct((n * chunk_b, width), BF16),
        ),
        in_specs=[smem] * 3 + [hbm] * 8,
        out_specs=(vmem,) * 3,
        scratch_shapes=[
            pltpu.VMEM((width, width), BF16),
            pltpu.VMEM((2 * width, width), BF16),
            pltpu.VMEM((1, width), F32),
            pltpu.VMEM((width, width), BF16),
            pltpu.VMEM((1, width), F32),
            dma((5,)),
            pltpu.VMEM((micros, rows, width), BF16),
            pltpu.VMEM(tile_weights.shape, BF16),
            pltpu.VMEM((micros, rows, width), BF16),
            pltpu.VMEM((blocks, size, width), BF16),
            pltpu.VMEM((micros, entries, size, width), BF16),
            pltpu.VMEM((micros, 2, sends, size, width), BF16),
            pltpu.VMEM((blocks, size, entries * size), BF16),
            pltpu.VMEM((entries * size, blocks * size), BF16),
            pltpu.VMEM((micros, rows, width), BF16),
            pltpu.VMEM((micros, rows, width), BF16),
            pltpu.VMEM((micros, rows, width), F32),
            pltpu.VMEM((micros, rows, 1), F32),
            pltpu.VMEM((micros, rows, width), F32),
            pltpu.VMEM((2, rows, width), F32),
            pltpu.VMEM((2, blocks, size, width), F32),
            pltpu.VMEM((rows, width), BF16),
            pltpu.VMEM((rows, width), BF16),
            pltpu.VMEM((rows, width), BF16),
            pltpu.VMEM((micros, 2, sends, size, width), BF16),
            pltpu.VMEM((micros, 2, sends, size, width), BF16),
            pltpu.VMEM((n * chunk_a, width), F32),
            pltpu.VMEM((n * chunk_b, width), F32),
            pltpu.VMEM((n * chunk_a, width), BF16),
            pltpu.VMEM((n - 1, chunk_a, width), BF16),
            pltpu.VMEM((n * chunk_b, width), BF16),
            pltpu.VMEM((n - 1, chunk_b, width), BF16),
            dma(()),
            dma((micros,)),
            dma(()),
            dma((micros, 2)),
            dma((micros, 2)),
            dma((micros, 2)),
            dma((micros, 2)),
            dma((micros, parts)),
            dma((micros, parts)),
        ]
        + [dma((n - 1,))] * 8,
        compiler_params=pltpu.CompilerParams(
            collective_id=0, has_side_effects=True, vmem_limit_bytes=40 * 1024 * 1024
        ),
    )(
        tile_source.T,
        tile_count,
        send_blocks[0],
        node_latents[0],
        cotangent,
        tile_weights,
        w_message[0],
        w_first[0],
        bias_first,
        w_second[0],
        norm_gain,
    )
    grads, message, first, bias, second, gain = pl.pallas_call(
        unpack,
        out_shape=(
            jax.ShapeDtypeStruct((micros, rows, width), BF16),
            jax.ShapeDtypeStruct((width, width), F32),
            jax.ShapeDtypeStruct((2 * width, width), F32),
            jax.ShapeDtypeStruct((1, width), F32),
            jax.ShapeDtypeStruct((width, width), F32),
            jax.ShapeDtypeStruct((1, width), F32),
        ),
        in_specs=[vmem, vmem, vmem],
        out_specs=(anywhere,) + (vmem,) * 5,
        scratch_shapes=[dma(())],
        compiler_params=pltpu.CompilerParams(vmem_limit_bytes=8 * 1024 * 1024),
    )(grads, packed_a, packed_b)
    return (grads[None], message[None], first[None], bias, second[None], gain)


def solution(mesh):
    return jax.shard_map(
        functools.partial(per_device, mesh.shape["dom"], mesh.shape["section"]),
        mesh=mesh,
        in_specs=(
            P("section", None, "dom", None),
            P(None, "dom", None),
            P("dom", None, None, None),
            P("dom", None),
            P("dom"),
            P("dom", None, None),
            P("section", None, None),
            P("section", None, None),
            P("section", None),
            P("section", None, None),
            P("section", None),
        ),
        out_specs=(
            P("section", None, "dom", None),
            P("section", None, None),
            P("section", None, None),
            P("section", None),
            P("section", None, None),
            P("section", None),
        ),
        check_vma=False,
    )
```

time: 88.2 us -> 80 us (0.907)
  Pallas kernels: 79.7 us -> 72.2 us
    pallas_call x1 -> x2, Pallas kernels: 79.7 us -> 72.2 us  [the longest x1 70.5 us: per_device(): pl.pallas_call(functools.partial(kernel, n, sections, (chunk_a, chunk_b),...]
    reshape x2 -> x0, local copies, waits for them, and re-layouts: 1.18 us -> none  [the longest x1 0.59 us: per_device(): tile_source.reshape(-1)]
    unnamed x21 -> x22, local copies, waits for them, and re-layouts: 6.32 us -> 6.72 us
where the time goes in v1:
time: 80 us; the launch traced here: 79.6 us
  Pallas kernels  72.2 us (90%)
  local copies, waits for them, and re-layouts  6.72 us (8%)
    pallas_call x1, Pallas kernels, per_device(): pl.pallas_call(functools.partial(kernel, n, sections, (chunk_a, chunk_b),...  70.5 us
    unnamed x22, local copies, waits for them, and re-layouts  6.72 us
    pallas_call x1, Pallas kernels, per_device(): pl.pallas_call(unpack, out_shape=(jax.ShapeDtypeStruct((micros, rows, wid...  1.68 us

profile of v1, /device:TPU:0, one launch (start us, length us, event | category | flops | bytes accessed | tf_op | source)
XLA Modules:
  0.0 79.6 jit_solution(4529408332895575738)
XLA Ops:
  0.6 0.0 copy-start.9
  0.6 0.0 copy-start.10
  0.7 0.0 copy-start.6
  0.7 0.0 copy-start.7
  0.7 0.0 copy-start.8
  0.7 0.6 copy-done.9
  1.3 0.0 copy-done.10
  1.3 0.0 copy-done.6
  1.4 0.0 copy-done.7
  1.4 0.0 copy-done.8
  1.4 0.0 copy-start
  1.4 1.2 %copy-done = bf16[1,4,1024,128]{3,2,1,0:T(8,128)(2,1)S(1)} copy-done((bf16[1,4,1024,128]{3,2,1,0:T(8,128)(2,1)S(1)}, bf16[1,4,1024,128]{3,2,1,0:T(8,128)(2,1)}, u32[]{:S(2)}) %copy-start) | copy-done | bytes 1048600
  2.6 0.0 copy-start.1
  2.6 1.2 %copy-done.1 = bf16[4,1024,128]{2,1,0:T(8,128)(2,1)S(1)} copy-done((bf16[4,1024,128]{2,1,0:T(8,128)(2,1)S(1)}, bf16[4,1024,128]{2,1,0:T(8,128)(2,1)}, u32[]{:S(2)}) %copy-start.1) | copy-done | bytes 1048600
  3.8 0.0 copy-start.2
  3.8 1.2 %copy-done.2 = bf16[8,4,128,128]{3,2,1,0:T(8,128)(2,1)S(1)} copy-done((bf16[8,4,128,128]{3,2,1,0:T(8,128)(2,1)S(1)}, bf16[8,4,128,128]{3,2,1,0:T(8,128)(2,1)}, u32[]{:S(2)}) %copy-start.2) | copy-done | bytes 1048600
  5.0 0.0 copy-start.3
  5.0 0.8 %copy-done.3 = bf16[1,256,128]{2,1,0:T(8,128)(2,1)S(1)} copy-done((bf16[1,256,128]{2,1,0:T(8,128)(2,1)S(1)}, bf16[1,256,128]{2,1,0:T(8,128)(2,1)}, u32[]{:S(2)}) %copy-start.3) | copy-done | bytes 65560
  5.9 0.0 copy-start.4
  5.9 0.8 copy-done.4
  6.6 0.0 copy-start.5
  6.6 0.8 copy-done.5
  7.4 70.5 %shard_map.154 = (bf16[4,1024,128]{2,1,0:T(8,128)(2,1)S(1)}, bf16[512,128]{1,0:T(8,128)(2,1)S(1)}, bf16[128,128]{1,0:T(8,128)(2,1)S(1)}) custom-call(s32[4,8]{1,0:T(4,128)S(1)} %bitcast.14, s32[8]{0:T(128)S(1)} %copy-done.8, s32[2,2]{1,0:T(2,128)S(1)} %bitcast.15, bf16[4,1024,128]{2,1,0:T(8,128)(2,1)S(1)} %bitcast.10, bf16[4,1024,128]{2,1,0:T(8,128)(2,1)S(1)} %copy-done.1, ...), custom_call_target="tpu_custom_call" | custom-call | tf_op jit(solution)/shard_map/pallas_call | solution.py:471
  77.9 1.7 %shard_map.155 = (bf16[4,1024,128]{2,1,0:T(8,128)(2,1)}, f32[128,128]{1,0:T(8,128)}, f32[256,128]{1,0:T(8,128)}, f32[1,128]{1,0:T(1,128)}, f32[128,128]{1,0:T(8,128)}, /*index=5*/f32[1,128]{1,0:T(1,128)}) custom-call(bf16[4,1024,128]{2,1,0:T(8,128)(2,1)S(1)} %get-tuple-element.15.grads_ref, bf16[512,128]{1,0:T(8,128)(2,1)S(1)} %get-tuple-element.16.a_ref, ...), custom_call_target="tpu_custom_call" | custom-call | tf_op jit(solution)/shard_map/pallas_call | solution.py:540
Async XLA Ops:
  0.6 0.7 copy-start.9
  0.6 0.7 copy-start.10
  0.7 0.7 copy-start.6
  0.7 0.7 copy-start.7
  0.7 0.7 copy-start.8
  1.4 1.2 %copy-start = (bf16[1,4,1024,128]{3,2,1,0:T(8,128)(2,1)S(1)}, bf16[1,4,1024,128]{3,2,1,0:T(8,128)(2,1)}, u32[]{:S(2)}) copy-start(bf16[1,4,1024,128]{3,2,1,0:T(8,128)(2,1)} %param.11) | copy-start | bytes 3145732
  2.6 1.2 %copy-start.1 = (bf16[4,1024,128]{2,1,0:T(8,128)(2,1)S(1)}, bf16[4,1024,128]{2,1,0:T(8,128)(2,1)}, u32[]{:S(2)}) copy-start(bf16[4,1024,128]{2,1,0:T(8,128)(2,1)} %cotangent_ref.1) | copy-start | bytes 3145732
  3.8 1.2 %copy-start.2 = (bf16[8,4,128,128]{3,2,1,0:T(8,128)(2,1)S(1)}, bf16[8,4,128,128]{3,2,1,0:T(8,128)(2,1)}, u32[]{:S(2)}) copy-start(bf16[8,4,128,128]{3,2,1,0:T(8,128)(2,1)} %tiles_hbm.1) | copy-start | bytes 3145732
  5.0 0.8 %copy-start.3 = (bf16[1,256,128]{2,1,0:T(8,128)(2,1)S(1)}, bf16[1,256,128]{2,1,0:T(8,128)(2,1)}, u32[]{:S(2)}) copy-start(bf16[1,256,128]{2,1,0:T(8,128)(2,1)} %param.18) | copy-start | bytes 196612
  5.9 0.8 copy-start.4
  6.6 0.8 copy-start.5

commit v2 on v1

--- a/solution.py
+++ b/solution.py
@@ -12,7 +12,7 @@
 MESH = pl.DeviceIdType.MESH
 F32 = jnp.float32
 BF16 = jnp.bfloat16
-parts = 2
+parts = 1
 
 
 def mm(a, b):
@@ -522,7 +522,7 @@
         ]
         + [dma((n - 1,))] * 8,
         compiler_params=pltpu.CompilerParams(
-            collective_id=0, has_side_effects=True, vmem_limit_bytes=40 * 1024 * 1024
+            collective_id=0, has_side_effects=True, vmem_limit_bytes=56 * 1024 * 1024
         ),
     )(
         tile_source.T,
@@ -550,7 +550,6 @@
         in_specs=[vmem, vmem, vmem],
         out_specs=(anywhere,) + (vmem,) * 5,
         scratch_shapes=[dma(())],
-        compiler_params=pltpu.CompilerParams(vmem_limit_bytes=8 * 1024 * 1024),
     )(grads, packed_a, packed_b)
     return (grads[None], message[None], first[None], bias, second[None], gain)
 

time: 80 us -> 75.2 us (0.940)
  local copies, waits for them, and re-layouts: 6.72 us -> 0 us
  Pallas kernels: 72.2 us -> 74.4 us
    unnamed x22 -> x0, local copies, waits for them, and re-layouts: 6.72 us -> none
    pallas_call x1, Pallas kernels: 1.68 us -> 2.98 us  [per_device(): pl.pallas_call(unpack, out_shape=(jax.ShapeDtypeStruct((micros, rows, wid...]
    pallas_call x1, Pallas kernels: 70.5 us -> 71.4 us  [per_device(): pl.pallas_call(functools.partial(kernel, n, sections, (chunk_a, chunk_b),...]
where the time goes in v2:
time: 75.2 us; the launch traced here: 75 us
  Pallas kernels  74.4 us (99%)
    pallas_call x1, Pallas kernels, per_device(): pl.pallas_call(functools.partial(kernel, n, sections, (chunk_a, chunk_b),...  71.4 us
    pallas_call x1, Pallas kernels, per_device(): pl.pallas_call(unpack, out_shape=(jax.ShapeDtypeStruct((micros, rows, wid...  2.98 us

profile of v2, /device:TPU:0, one launch (start us, length us, event | category | flops | bytes accessed | tf_op | source)
XLA Modules:
  0.0 75.0 jit_solution(4437293453457880799)
XLA Ops:
  0.6 71.4 %shard_map.154 = (bf16[4,1024,128]{2,1,0:T(8,128)(2,1)}, bf16[512,128]{1,0:T(8,128)(2,1)}, bf16[128,128]{1,0:T(8,128)(2,1)}) custom-call(s32[4,8]{1,0:T(4,128)} %bitcast.14, s32[8]{0:T(128)} %count_ref.1, s32[2,2]{1,0:T(2,128)} %bitcast.15, bf16[4,1024,128]{2,1,0:T(8,128)(2,1)} %bitcast.10, bf16[4,1024,128]{2,1,0:T(8,128)(2,1)} %cotangent_ref.1, ...), custom_call_target="tpu_custom_call" | custom-call | tf_op jit(solution)/shard_map/pallas_call | solution.py:471
  72.0 3.0 %shard_map.155 = (bf16[4,1024,128]{2,1,0:T(8,128)(2,1)}, f32[128,128]{1,0:T(8,128)}, f32[256,128]{1,0:T(8,128)}, f32[1,128]{1,0:T(1,128)}, f32[128,128]{1,0:T(8,128)}, /*index=5*/f32[1,128]{1,0:T(1,128)}) custom-call(bf16[4,1024,128]{2,1,0:T(8,128)(2,1)} %get-tuple-element.15.grads_ref, bf16[512,128]{1,0:T(8,128)(2,1)} %get-tuple-element.16.a_ref, ...), custom_call_target="tpu_custom_call" | custom-call | tf_op jit(solution)/shard_map/pallas_call | solution.py:540
